TPU v7x, 32 devices: a whole 2x2x4 slice. The times are simulated.
32 devices in a mesh: req: 8 (over z, y), tp: 4 (over x, core).
Axes of the slice: x: 2, y: 2, z: 4, core: 2. Of those that a mesh axis runs over, the one named last changes fastest.
Arguments:
- tokens: bfloat16 [8192, 1792], P(('req', 'tp')), may hold values from -6 to 6
- norm_gain: float32 [1792], replicated, may hold values from 0.25 to 1.75
- ffn_gain: float32 [1792], replicated, may hold values from 0.25 to 1.75
- mix_weight: bfloat16 [1792, 4, 1792], P('req', None, 'tp'), may hold values from -0.125 to 0.125
- out_weight: bfloat16 [1792, 1792], P('tp', 'req'), may hold values from -0.125 to 0.125
- ffn_weight: bfloat16 [1792, 2, 7168], P('req', None, 'tp'), may hold values from -0.125 to 0.125
- down_weight: bfloat16 [7168, 1792], P('tp', 'req'), may hold values from -0.0625 to 0.0625
- conv_taps: float32 [3, 1792], P(None, 'tp'), may hold values from -3 to 3
- past_cache: bfloat16 [8, 2, 64, 1792], P('req', None, None, 'tp'), may hold values from -210 to 210
- cached_len: int32 [8], P('req'), may hold values from 0 to 8192, as said below
Outputs:
- layer_out: bfloat16 [8192, 1792], P(('req', 'tp'))
- new_cache: bfloat16 [8, 2, 64, 1792], P('req', None, None, 'tp')
Inputs may be any that keep to these rules, and one draw needn't show every extreme that they name: `cached_len`: one request has exactly 8192 cached positions and another fewer than 64.
All inputs are finite; a program needn't handle non-finite values.
Results may differ from a plain program's by a relative error of at most 0.02.
Values may be sent and summed in bfloat16 or wider, within the bound.
A program may use at most 128 MiB of HBM per device.

v0:
```python
import math

import jax
import jax.numpy as jnp
from jax import lax
from jax.sharding import PartitionSpec as P

HD = 112
WIN = 64


def normed(row_vals, gain):
    floats = row_vals.astype(jnp.float32)
    scaled = floats * lax.rsqrt(jnp.mean(floats * floats, axis=-1, keepdims=True) + 1e-05)
    return (scaled * gain).astype(jnp.bfloat16)


def window_attend(queries, key_rows, value_rows, length, window):
    row_count, head_count, head_size = queries.shape
    block_rows = min(512, row_count)
    score_scale = 1.0 / math.sqrt(head_size)

    def one_block(block_index):
        begin_row = block_index * block_rows
        query_block = lax.dynamic_slice_in_dim(queries, begin_row, block_rows, 0)
        key_block = lax.dynamic_slice_in_dim(key_rows, begin_row, block_rows + window, 0)
        value_block = lax.dynamic_slice_in_dim(value_rows, begin_row, block_rows + window, 0)
        scores = (
            jnp.einsum("qhd,khd->hqk", query_block, key_block, preferred_element_type=jnp.float32)
            * score_scale
        )
        row_ids = begin_row + jnp.arange(block_rows, dtype=jnp.int32)[:, None]
        col_ids = begin_row + jnp.arange(block_rows + window, dtype=jnp.int32)[None, :]
        usable = (col_ids > row_ids) & (col_ids <= row_ids + window) & (col_ids >= window - length)
        scores = jnp.where(usable[None], scores, -1e30)
        row_max = jnp.max(scores, axis=-1, keepdims=True)
        exponent = jnp.exp(scores - row_max)
        weights = (exponent / jnp.sum(exponent, axis=-1, keepdims=True)).astype(jnp.bfloat16)
        return jnp.einsum("hqk,khd->qhd", weights, value_block, preferred_element_type=jnp.float32)

    blocks = lax.map(one_block, jnp.arange(row_count // block_rows, dtype=jnp.int32))
    return blocks.reshape(row_count, head_count, head_size)


def mix_request(projected, cache_rows, length, tap_table, window, head_size):
    row_count, feat_width = (projected.shape[0], projected.shape[2])
    time_order = (length + jnp.arange(window, dtype=jnp.int32)) % window
    earlier = cache_rows[:, time_order]
    key_rows = jnp.concatenate([earlier[0], projected[:, 1]], axis=0)
    value_rows = jnp.concatenate([earlier[1], projected[:, 2]], axis=0)
    head_count = feat_width // head_size
    attended = window_attend(
        projected[:, 0].reshape(row_count, head_count, head_size),
        key_rows.reshape(-1, head_count, head_size),
        value_rows.reshape(-1, head_count, head_size),
        length,
        window,
    ).reshape(row_count, feat_width)
    positions = jnp.arange(window + row_count, dtype=jnp.int32)
    alive_mask = (positions >= window - length)[:, None]
    masked_values = jnp.where(alive_mask, value_rows.astype(jnp.float32), jnp.float32(0.0))
    tap_count = tap_table.shape[0]
    convolved = jnp.zeros((row_count, feat_width), jnp.float32)
    for tap_index in range(tap_count):
        begin_row = window - (tap_count - 1) + tap_index
        convolved = (
            convolved + tap_table[tap_index] * masked_values[begin_row : begin_row + row_count]
        )
    mixed_heads = (attended + projected[:, 3].astype(jnp.float32) * convolved).astype(jnp.bfloat16)
    slot_source = (
        row_count - window + (jnp.arange(window, dtype=jnp.int32) - length - row_count) % window
    )
    renewed = jnp.stack([projected[:, 1], projected[:, 2]])[:, slot_source]
    return (mixed_heads, renewed)


def add_rows(left, shard_piece):
    return jnp.dot(
        left, shard_piece.reshape(shard_piece.shape[0], -1), preferred_element_type=jnp.float32
    )


def local(
    tokens,
    norm_gain,
    ffn_gain,
    mix_weight,
    out_weight,
    ffn_weight,
    down_weight,
    conv_taps,
    past_cache,
    cached_len,
):
    feat_width = mix_weight.shape[2]
    ffn_width = ffn_weight.shape[2]
    normed_all = lax.all_gather(normed(tokens, norm_gain), "tp", axis=0, tiled=True)
    row_total = normed_all.shape[0]
    projected = add_rows(normed_all, lax.all_gather(mix_weight, "req", axis=0, tiled=True))
    projected = projected.astype(jnp.bfloat16).reshape(row_total, 4, feat_width)
    mixed_heads, renewed = mix_request(projected, past_cache[0], cached_len[0], conv_taps, WIN, HD)
    out_columns = lax.all_gather(out_weight, "req", axis=1, tiled=True)
    attn_part = lax.psum_scatter(
        jnp.dot(mixed_heads, out_columns, preferred_element_type=jnp.float32).astype(jnp.bfloat16),
        "tp",
        scatter_dimension=0,
        tiled=True,
    ).astype(jnp.float32)
    residual = (tokens.astype(jnp.float32) + attn_part).astype(jnp.bfloat16)
    ffn_in = lax.all_gather(normed(residual, ffn_gain), "tp", axis=0, tiled=True)
    gate_up = add_rows(ffn_in, lax.all_gather(ffn_weight, "req", axis=0, tiled=True))
    down_columns = lax.all_gather(down_weight, "req", axis=1, tiled=True)
    activated = (jax.nn.silu(gate_up[:, :ffn_width]) * gate_up[:, ffn_width:]).astype(jnp.bfloat16)
    ffn_part = lax.psum_scatter(
        jnp.dot(activated, down_columns, preferred_element_type=jnp.float32).astype(jnp.bfloat16),
        "tp",
        scatter_dimension=0,
        tiled=True,
    ).astype(jnp.float32)
    layer_out = (residual.astype(jnp.float32) + ffn_part).astype(jnp.bfloat16)
    return (layer_out, renewed[None])


def solution(mesh):
    in_specs = (
        P(("req", "tp"), None),
        P(),
        P(),
        P("req", None, "tp"),
        P("tp", "req"),
        P("req", None, "tp"),
        P("tp", "req"),
        P(None, "tp"),
        P("req", None, None, "tp"),
        P("req"),
    )
    out_specs = (P(("req", "tp"), None), P("req", None, None, "tp"))
    return jax.shard_map(local, mesh=mesh, in_specs=in_specs, out_specs=out_specs, check_vma=False)
```

profile of v0, /device:TPU:1, one launch (start us, length us, event | category | flops | bytes accessed | tf_op | source)
XLA Modules:
  0.0 666.4 jit_solution(10254516377275731987)
XLA Ops:
  9.4 1.9 fusion.19
  14.6 109.3 %all-gather.9.cloned.1.call-done = bf16[1792,4,448]{2,1,0:T(4,128)(2,1)} async-done(((bf16[224,4,448]{2,1,0:T(4,128)(2,1)}), bf16[1792,4,448]{2,1,0:T(4,128)(2,1)}) %all-gather.9.cloned.1.call-update) | async-done | bytes 6422544 | tf_op jit(solution)/shard_map/all_gather | solution.py:99
  123.9 12.9 %copy.43 = bf16[1792,4,448]{0,2,1:T(8,128)(2,1)} copy(bf16[1792,4,448]{2,1,0:T(4,128)(2,1)} %all-gather.9.cloned.1.call-done) | data formatting | bytes 12845056 | tf_op jit(solution)/shard_map/all_gather | solution.py:99
  136.8 19.8 %all-gather.7.cloned.1.call-done = bf16[1024,1792]{1,0:T(8,128)(2,1)} async-done(((bf16[256,1792]{1,0:T(8,128)(2,1)}), bf16[1024,1792]{1,0:T(8,128)(2,1)}) %all-gather.7.cloned.1.call-update) | async-done | bytes 3670032 | tf_op jit(solution)/shard_map/all_gather | solution.py:97
  156.6 11.7 %convolution_convert_fusion.1 = bf16[1024,1792]{1,0:T(8,128)(2,1)} fusion(bf16[1024,1792]{1,0:T(8,128)(2,1)} %all-gather.7.cloned.1.call-done, bf16[1792,1792]{0,1:T(8,128)(2,1)} %bitcast.63), kind=kOutput, calls=%fused_computation.28 | convolution fusion | flops 6578503680 | bytes 13762560 | tf_op jit(solution)/shard_map/dot_general | solution.py:78
  168.3 5.9 copy.44
  174.2 3.9 slice_bitcast_fusion.2
  180.1 53.7 %while.12 = (s32[]{:T(128)}, f32[2,512,4,112]{1,0,3,2:T(2,128)}, s32[2]{0:T(128)S(1)}, bf16[1088,4,112]{0,2,1:T(8,128)(2,1)}, s32[]{:T(128)}, /*index=5*/bf16[10...) while((s32[]{:T(128)}, f32[2,512,4,112]{1,0,3,2:T(2,128)}, ...), condition=%wide.region_4.5_spmd, body=%wide.region_1.4_spmd.sunk | while | flops 539102464 | bytes 25687912 | solution.py:41
  181.5 2.3 fusion.58
  184.2 2.6 fusion.59
  186.8 1.9 fusion.60
  189.7 17.3 %dynamic_update_slice.7 = f32[2,512,4,112]{1,0,3,2:T(2,128)} dynamic-update-slice(f32[2,512,4,112]{1,0,3,2:T(2,128)} %get-tuple-element.187, f32[1,512,4,112]{1,0,3,2:T(1,128)S(1)} %copy.65, s32[]{:T(128)} %get-tuple-element.186, s32[]{:T(128)} %constant.82.clone.1..sunk, s32[]{:T(128)} %constant.82.clone.1..sunk, s32[]{:T(128)} %constant.82.clone.1..sunk) | dynamic-update-slice | bytes 1835012 | tf_op jit(solution)/shard_map/while/body/jit(dynamic_update_index_in_dim)/dynamic_update_slice | solution.py:41
  208.3 2.3 fusion.58
  211.1 2.6 fusion.59
  213.7 1.9 fusion.60
  216.5 17.3 %dynamic_update_slice.7 = f32[2,512,4,112]{1,0,3,2:T(2,128)} dynamic-update-slice(f32[2,512,4,112]{1,0,3,2:T(2,128)} %get-tuple-element.187, f32[1,512,4,112]{1,0,3,2:T(1,128)S(1)} %copy.65, s32[]{:T(128)} %get-tuple-element.186, s32[]{:T(128)} %constant.82.clone.1..sunk, s32[]{:T(128)} %constant.82.clone.1..sunk, s32[]{:T(128)} %constant.82.clone.1..sunk) | dynamic-update-slice | bytes 1835012 | tf_op jit(solution)/shard_map/while/body/jit(dynamic_update_index_in_dim)/dynamic_update_slice | solution.py:41
  233.8 3.2 copy.60
  237.6 8.1 %convolution_convert_fusion.2 = bf16[1024,1792]{1,0:T(8,128)(2,1)} fusion(bf16[448,1792]{0,1:T(8,128)(2,1)} %all-gather.11.cloned.1.call-done, f32[1024,448]{0,1:T(8,128)} %bitcast.67, f32[1088,448]{0,1:T(8,128)S(1)} %convert_select_fusion, bf16[1024,4,448]{0,2,1:T(8,128)(2,1)} %bitcast.62, f32[448]{0:T(512)S(1)} %bitcast.75, f32[448]{0:T(512)S(1)} %bitcast.76, ...), kind=kOutput, calls=%fused_computation.29 | convolution fusion | flops 1650130944 | bytes 13768704 | tf_op jit(solution)/shard_map/dot_general | solution.py:104
  246.4 40.3 %reduce-scatter.3.cloned.1.call-done = bf16[256,1792]{1,0:T(8,128)(2,1)} async-done(((bf16[1024,1792]{1,0:T(8,128)(2,1)}), bf16[256,1792]{1,0:T(8,128)(2,1)}) %reduce-scatter.3.cloned.1.call-update) | async-done | bytes 917520 | tf_op jit(solution)/shard_map/reduce_scatter | solution.py:103
  286.7 1.6 fusion.21
  290.5 177.7 %all-gather.15.cloned.1.call-done = bf16[1792,2,1792]{2,1,0:T(2,128)(2,1)} async-done(((bf16[224,2,1792]{2,1,0:T(2,128)(2,1)}), bf16[1792,2,1792]{2,1,0:T(2,128)(2,1)}) %all-gather.15.cloned.1.call-update) | async-done | bytes 12845072 | tf_op jit(solution)/shard_map/all_gather | solution.py:111
  468.3 12.7 %copy.61 = bf16[224,8,2,1792]{3,1,2,0:T(8,128)(2,1)} copy(bf16[224,8,2,1792]{3,2,1,0:T(2,128)(2,1)} %bitcast.59) | data formatting | bytes 25690112
  481.0 19.3 %all-gather.13.cloned.1.call-done = bf16[1024,1792]{1,0:T(8,128)(2,1)} async-done(((bf16[256,1792]{1,0:T(8,128)(2,1)}), bf16[1024,1792]{1,0:T(8,128)(2,1)}) %all-gather.13.cloned.1.call-update) | async-done | bytes 3670032 | tf_op jit(solution)/shard_map/all_gather | solution.py:110
  500.3 20.6 %fusion.42 = f32[1024,3584]{1,0:T(8,128)} fusion(bf16[1024,1792]{1,0:T(8,128)(2,1)} %all-gather.13.cloned.1.call-done, bf16[1792,3584]{1,0:T(8,128)(2,1)} %bitcast.60), kind=kOutput, calls=%fused_computation.85 | convolution fusion | flops 13153337344 | bytes 31195136 | tf_op jit(solution)/shard_map/dot_general | solution.py:78
  520.9 81.7 %all-gather.17.cloned.1.call-done = bf16[1792,1792]{0,1:T(8,128)(2,1)} async-done(((bf16[1792,224]{0,1:T(8,128)(2,1)}), bf16[1792,1792]{0,1:T(8,128)(2,1)}) %all-gather.17.cloned.1.call-update) | async-done | bytes 6422544 | tf_op jit(solution)/shard_map/all_gather | solution.py:112
  602.5 14.3 %convolution_convert_fusion = bf16[1024,1792]{1,0:T(8,128)(2,1)} fusion(bf16[1792,1792]{0,1:T(8,128)(2,1)} %all-gather.17.cloned.1.call-done, f32[1024,3584]{1,0:T(8,128)} %fusion.42), kind=kOutput, calls=%fused_computation.27 | convolution fusion | flops 6589513728 | bytes 24772608 | tf_op jit(solution)/shard_map/dot_general | solution.py:115
  616.8 4.6 copy.50
  621.4 6.0 copy.51
  627.5 6.8 %pad_maximum_fusion = bf16[2,1024,448]{2,0,1:T(2,128)(2,1)} fusion(bf16[1,1024,448]{2,0,1:T(2,128)(2,1)} %copy.51, bf16[1,1024,448]{2,0,1:T(2,128)(2,1)S(1)} %copy.50), kind=kLoop, calls=%fused_computation.36 | loop fusion | flops 3670016 | bytes 3670016 | tf_op jit(solution)/shard_map/stack | solution.py:73
  634.3 2.6 gather_fusion.1
  637.6 19.3 %reduce-scatter.5.cloned.1.call-done = bf16[256,1792]{1,0:T(8,128)(2,1)} async-done(((bf16[1024,1792]{1,0:T(8,128)(2,1)}), bf16[256,1792]{1,0:T(8,128)(2,1)}) %reduce-scatter.5.cloned.1.call-update) | async-done | bytes 917520 | tf_op jit(solution)/shard_map/reduce_scatter | solution.py:114
  656.8 2.7 fusion.24
  (64 shorter events, 14.6 us)
Async XLA Ops:
  7.2 2.3 copy-start
  7.2 116.7 %all-gather.9.cloned.1.call-start = ((), (), s32[]{:S(2)}) async-start(), calls=%async_computation.3 | async-start | bytes 8257536 | tf_op jit(solution)/shard_map/all_gather | solution.py:99
  7.2 4.2 copy-start.3
  7.9 5.1 copy-start.4
  7.9 148.7 %all-gather.7.cloned.1.call-start = ((), (), s32[]{:S(2)}) async-start(), calls=%async_computation.2 | async-start | bytes 4587520 | tf_op jit(solution)/shard_map/all_gather | solution.py:97
  9.4 5.1 copy-start.6
  11.4 226.3 %all-gather.11.cloned.1.call-start = ((), (), s32[]{:S(2)}) async-start(), calls=%async_computation.4 | async-start | bytes 2064384 | tf_op jit(solution)/shard_map/all_gather | solution.py:102
  12.3 274.4 %reduce-scatter.3.cloned.1.call-start = ((), (), s32[]{:S(2)}) async-start(), calls=%async_computation.5 | async-start | bytes 4587520 | tf_op jit(solution)/shard_map/reduce_scatter | solution.py:103
  233.8 3.2 copy-start.2
  245.7 42.6 %copy-start.5 = (f32[1792]{0:T(1024)S(1)}, f32[1792]{0:T(1024)}, u32[]{:S(2)}) copy-start(f32[1792]{0:T(1024)} %param.14) | copy-start | bytes 21508
  245.7 222.5 %all-gather.15.cloned.1.call-start = ((), (), s32[]{:S(2)}) async-start(), calls=%async_computation.7 | async-start | bytes 14450688 | tf_op jit(solution)/shard_map/all_gather | solution.py:111
  246.3 254.0 %all-gather.13.cloned.1.call-start = ((), (), s32[]{:S(2)}) async-start(), calls=%async_computation.6 | async-start | bytes 4587520 | tf_op jit(solution)/shard_map/all_gather | solution.py:110
  286.7 1.7 copy-start.1
  289.7 312.8 %all-gather.17.cloned.1.call-start = ((), (), s32[]{:S(2)}) async-start(), calls=%async_computation.8 | async-start | bytes 7225344 | tf_op jit(solution)/shard_map/all_gather | solution.py:112
  290.5 366.4 %reduce-scatter.5.cloned.1.call-start = ((), (), s32[]{:S(2)}) async-start(), calls=%async_computation.9 | async-start | bytes 4587520 | tf_op jit(solution)/shard_map/reduce_scatter | solution.py:114
Sparse Core Ops, SparseCore 0:
  10.2 113.6 all-gather.8
  126.0 30.4 all-gather.6
  158.8 44.8 all-gather.10
  245.8 40.8 reduce-scatter.2
  289.0 179.2 all-gather.14
  469.8 30.4 all-gather.12
  502.7 99.7 all-gather.16
  616.9 39.8 reduce-scatter.4
where the time goes:
time: 671 us; the launch traced here: 666 us
  waiting for transfers between devices  469 us (70%)
  local copies, waits for them, and re-layouts  92.8 us (14%)
  matrix products  63 us (9%)
  other arithmetic  24.3 us (4%)
  between operations  15 us (2%)
    all_gather x1, waiting for transfers between devices, local(): lax.all_gather(ffn_weight, 'req', axis=0, tiled=True)  178 us
    all_gather x1, waiting for transfers between devices, local(): lax.all_gather(mix_weight, 'req', axis=0, tiled=True)  109 us
    all_gather x1, waiting for transfers between devices, local(): down_columns = lax.all_gather(down_weight, 'req', axis=1, tiled=True)  81.7 us
    reduce_scatter x1, waiting for transfers between devices, local(): lax.psum_scatter(jnp.dot(mixed_heads, out_columns, preferred_element_type...  40.3 us
    dynamic_update_slice x4, local copies, waits for them, and re-layouts, window_attend(): lax.map(one_block, jnp.arange(row_count // block_rows, dtype=jnp.int32))  36.4 us
    dot_general x2, matrix products, add_rows(): jnp.dot(left, shard_piece.reshape(shard_piece.shape[0], -1), preferred_el...  32.2 us
    all_gather x1, waiting for transfers between devices, local(): lax.all_gather(normed(tokens, norm_gain), 'tp', axis=0, tiled=True)  19.8 us
    all_gather x1, waiting for transfers between devices, local(): lax.all_gather(normed(residual, ffn_gain), 'tp', axis=0, tiled=True)  19.3 us
  transfers between devices with their start and end apart: 8, of which 7 were waited for; matrix products, arithmetic and copies ran while one was open for 23% of the time, Pallas kernels for 0%

commit v1 on v0

--- a/solution.py
+++ b/solution.py
@@ -1,8 +1,12 @@
+import functools
 import math
 
 import jax
 import jax.numpy as jnp
+import numpy as np
 from jax import lax
+from jax.experimental import pallas as pl
+from jax.experimental.pallas import tpu as pltpu
 from jax.sharding import PartitionSpec as P
 
 HD = 112
@@ -120,6 +124,515 @@
     layer_out = (residual.astype(jnp.float32) + ffn_part).astype(jnp.bfloat16)
     return (layer_out, renewed[None])
 
+MESH = pl.DeviceIdType.MESH
+
+
+def ring_spot(req_index, ring_size):
+    z_index, y_index = req_index // 2, req_index % 2
+    return z_index * (1 - y_index) + (ring_size - 1 - z_index) * y_index
+
+
+def spot_req(spot, ring_size):
+    side = spot // (ring_size // 2)
+    return 2 * (spot * (1 - side) + (ring_size - 1 - spot) * side) + side
+
+
+def layer_kernel(
+    ring_size,
+    group_size,
+    window,
+    head_count,
+    head_size,
+    tokens_ref,
+    norm_gain_ref,
+    ffn_gain_ref,
+    taps_ref,
+    cache_ref,
+    length_ref,
+    spread_ref,
+    mix_ref,
+    out_ref,
+    ffn_ref,
+    down_ref,
+    ffn_sum_ref,
+    residual_ref,
+    renewed_ref,
+    mix_all,
+    out_all,
+    ffn_all,
+    down_all,
+    normed_all,
+    ffn_in_all,
+    key_rows,
+    value_rows,
+    mixed,
+    attn_got,
+    shared,
+    down_part,
+    down_got,
+    ring_send,
+    ring_recv,
+    own_sem,
+    gather_send,
+    gather_recv,
+    attn_send,
+    attn_recv,
+    ffn_send,
+    ffn_recv,
+    down_send,
+    down_recv,
+):
+    my_req, my_tp = lax.axis_index("req"), lax.axis_index("tp")
+    spot = ring_spot(my_req, ring_size)
+    right = spot_req((spot + 1) % ring_size, ring_size)
+    left = spot_req((spot + ring_size - 1) % ring_size, ring_size)
+    own_rows, width = tokens_ref.shape
+    row_total = own_rows * group_size
+    shard_rows = mix_ref.shape[0]
+    half = shard_rows // 2
+    feat_width = out_all.shape[1]
+    hidden = ffn_all.shape[1] // 2
+    half_cols = mix_ref.shape[1] // 2
+    wide = head_count * 128
+    last = ring_size - 2
+
+    streams = [
+        (out_ref, out_all, 0, feat_width),
+        (mix_ref, mix_all, 0, half_cols),
+        (mix_ref, mix_all, half_cols, half_cols),
+        (ffn_ref, ffn_all, 0, hidden),
+        (ffn_ref, ffn_all, hidden, hidden),
+        (down_ref, down_all, 0, hidden // 2),
+        (down_ref, down_all, hidden // 2, hidden // 2),
+    ]
+    mix_phase, ffn_phase, down_phase = (0, 1, 2), (3, 4), (5, 6)
+
+    def shard_req(direction, step):
+        if direction == 0:
+            return spot_req((spot + ring_size - step) % ring_size, ring_size)
+        return spot_req((spot + step) % ring_size, ring_size)
+
+    def half_begin(direction, step):
+        return pl.multiple_of(shard_req(direction, step) * shard_rows + direction * half, 16)
+
+    def ring_copy(stream, direction, step, first):
+        source, whole, col_begin, col_count = streams[stream]
+        cols = pl.ds(col_begin, col_count)
+        place = whole.at[pl.ds(half_begin(direction, step), half), cols]
+        sem_index = (stream * 2 + direction) * (ring_size - 1) + step
+        return pltpu.make_async_remote_copy(
+            src_ref=source.at[pl.ds(direction * half, half), cols] if first else place,
+            dst_ref=place,
+            send_sem=ring_send.at[sem_index],
+            recv_sem=ring_recv.at[sem_index],
+            device_id={"req": left if direction else right},
+            device_id_type=MESH,
+        )
+
+    def ring_arrived(stream, direction, step):
+        _, whole, col_begin, col_count = streams[stream]
+        place = whole.at[
+            pl.ds(half_begin(direction, step + 1), half), pl.ds(col_begin, col_count)
+        ]
+        sem_index = (stream * 2 + direction) * (ring_size - 1) + step
+        pltpu.make_async_remote_copy(
+            src_ref=place,
+            dst_ref=place,
+            send_sem=ring_send.at[sem_index],
+            recv_sem=ring_recv.at[sem_index],
+            device_id={"req": left if direction else right},
+            device_id_type=MESH,
+        ).wait_recv()
+
+    def begin(phase):
+        for stream in phase:
+            for direction in range(2):
+                ring_copy(stream, direction, 0, True).start()
+
+    def tick(phase, step):
+        for stream in phase:
+            for direction in range(2):
+                ring_arrived(stream, direction, step - 1)
+                ring_copy(stream, direction, step, False).start()
+
+    def ticks(phase, low, high):
+        @pl.loop(low, high)
+        def _(step):
+            tick(phase, step)
+
+    def finish(phase):
+        for stream in phase:
+            for direction in range(2):
+                ring_arrived(stream, direction, last)
+
+    def own_copy(index):
+        source, whole = ((mix_ref, mix_all), (out_ref, out_all), (ffn_ref, ffn_all), (down_ref, down_all))[index]
+        begin_row = pl.multiple_of(my_req * shard_rows, 16)
+        return pltpu.make_async_copy(
+            source, whole.at[pl.ds(begin_row, shard_rows)], own_sem.at[index]
+        )
+
+    def peer(distance):
+        return (my_tp + distance) % group_size
+
+    def group_rows(member):
+        return pl.ds(pl.multiple_of(member * own_rows, 16), own_rows)
+
+    def gather_copy(whole, sends, recvs, distance):
+        rows = whole.at[group_rows(my_tp)]
+        return pltpu.make_async_remote_copy(
+            src_ref=rows,
+            dst_ref=rows,
+            send_sem=sends.at[distance - 1],
+            recv_sem=recvs.at[distance - 1],
+            device_id={"tp": peer(distance)},
+            device_id_type=MESH,
+        )
+
+    def gather_arrived(whole, sends, recvs, distance):
+        rows = whole.at[group_rows((my_tp + group_size - distance) % group_size)]
+        pltpu.make_async_remote_copy(
+            src_ref=rows,
+            dst_ref=rows,
+            send_sem=sends.at[distance - 1],
+            recv_sem=recvs.at[distance - 1],
+            device_id={"tp": peer(distance)},
+            device_id_type=MESH,
+        ).wait_recv()
+
+    def attn_copy(distance):
+        return pltpu.make_async_remote_copy(
+            src_ref=normed_all.at[group_rows(peer(distance))],
+            dst_ref=attn_got.at[distance - 1],
+            send_sem=attn_send.at[distance - 1],
+            recv_sem=attn_recv.at[distance - 1],
+            device_id={"tp": peer(distance)},
+            device_id_type=MESH,
+        )
+
+    def down_copy(distance, direction, step):
+        block = shard_req(direction, step) * 2 + direction
+        sem_index = ((distance - 1) * 2 + direction) * ring_size + step
+        return pltpu.make_async_remote_copy(
+            src_ref=down_part.at[block, group_rows(peer(distance))],
+            dst_ref=down_got.at[distance - 1, block],
+            send_sem=down_send.at[sem_index],
+            recv_sem=down_recv.at[sem_index],
+            device_id={"tp": peer(distance)},
+            device_id_type=MESH,
+        )
+
+    def rows_dot(a, b):
+        return lax.dot_general(
+            a, b, (((1,), (1,)), ((), ())), preferred_element_type=jnp.float32
+        )
+
+    barrier = pltpu.get_barrier_semaphore()
+    for neighbour in (left, right):
+        pl.semaphore_signal(
+            barrier, inc=1, device_id={"req": neighbour}, device_id_type=MESH
+        )
+    for distance in range(1, group_size):
+        pl.semaphore_signal(
+            barrier, inc=1, device_id={"tp": peer(distance)}, device_id_type=MESH
+        )
+    pl.semaphore_wait(barrier, 1 + group_size)
+
+    begin(mix_phase)
+    for index in range(4):
+        own_copy(index).start()
+    normed_all[group_rows(my_tp), :] = normed(tokens_ref[...], norm_gain_ref[...])
+    for distance in range(1, group_size):
+        gather_copy(normed_all, gather_send, gather_recv, distance).start()
+
+    length = length_ref[0]
+    row_ids = lax.broadcasted_iota(jnp.int32, (window, window), 0)
+    col_ids = lax.broadcasted_iota(jnp.int32, (window, window), 1)
+    slot_order = ((col_ids - row_ids - length) & (window - 1)) == 0
+    slot_order = jnp.where(slot_order, 1.0, 0.0).astype(jnp.bfloat16)
+    slot_back = ((row_ids - col_ids - length - row_total) & (window - 1)) == 0
+    slot_back = jnp.where(slot_back, 1.0, 0.0).astype(jnp.bfloat16)
+    spread_one = spread_ref[0:feat_width, 0:wide]
+    for part, rows_ref in ((0, key_rows), (1, value_rows)):
+        earlier = jnp.dot(slot_order, cache_ref[part], preferred_element_type=jnp.float32)
+        rows_ref[0:window, :] = jnp.dot(
+            earlier.astype(jnp.bfloat16), spread_one, preferred_element_type=jnp.float32
+        ).astype(jnp.bfloat16)
+
+    ticks(mix_phase, 1, last + 1)
+    begin(ffn_phase)
+    for distance in range(1, group_size):
+        gather_arrived(normed_all, gather_send, gather_recv, distance)
+    own_copy(0).wait()
+    own_copy(1).wait()
+    finish(mix_phase)
+
+    @pl.loop(0, mix_all.shape[1] // 256)
+    def _(tile):
+        cols = pl.ds(pl.multiple_of(tile * 256, 256), 256)
+        shared[:, cols] = jnp.dot(
+            normed_all[...], mix_all[:, cols], preferred_element_type=jnp.float32
+        ).astype(jnp.bfloat16)
+
+    block_rows = 128
+    key_count = block_rows + window
+    score_scale = 1.0 / math.sqrt(head_size)
+
+    def attend(block):
+        begin_row = pl.multiple_of(block * block_rows, 128)
+        rows = pl.ds(begin_row, block_rows)
+        left_half = jnp.dot(
+            shared[rows, 0 : 2 * feat_width], spread_ref[...], preferred_element_type=jnp.float32
+        ).astype(jnp.bfloat16)
+        right_half = jnp.dot(
+            shared[rows, 2 * feat_width : 4 * feat_width],
+            spread_ref[...],
+            preferred_element_type=jnp.float32,
+        )
+        new_rows = pl.ds(pl.multiple_of(block * block_rows + window, 64), block_rows)
+        key_rows[new_rows, :] = left_half[:, wide:]
+        value_rows[new_rows, :] = right_half[:, :wide].astype(jnp.bfloat16)
+        keys = key_rows[pl.ds(begin_row, key_count), :]
+        values = value_rows[pl.ds(begin_row, key_count), :]
+        query_ids = lax.broadcasted_iota(jnp.int32, (block_rows, key_count), 0)
+        key_ids = lax.broadcasted_iota(jnp.int32, (block_rows, key_count), 1)
+        usable = (
+            (key_ids > query_ids)
+            & (key_ids <= query_ids + window)
+            & (key_ids + begin_row >= window - length)
+        )
+        attended = []
+        for head in range(head_count):
+            cols = slice(head * 128, head * 128 + 128)
+            scores = rows_dot(left_half[:, cols], keys[:, cols]) * score_scale
+            scores = jnp.where(usable, scores, -1e30)
+            exponent = jnp.exp(scores - jnp.max(scores, axis=-1, keepdims=True))
+            weights = exponent / jnp.sum(exponent, axis=-1, keepdims=True)
+            attended.append(
+                jnp.dot(
+                    weights.astype(jnp.bfloat16),
+                    values[:, cols],
+                    preferred_element_type=jnp.float32,
+                )
+            )
+        attended = jnp.concatenate(attended, axis=1)
+        live_ids = lax.broadcasted_iota(jnp.int32, (key_count, wide), 0) + begin_row
+        live = jnp.where(live_ids >= window - length, values.astype(jnp.float32), 0.0)
+        tap_count = taps_ref.shape[0]
+        convolved = jnp.zeros((block_rows, wide), jnp.float32)
+        for tap in range(tap_count):
+            shift = tap_count - 1 - tap
+            moved = pltpu.roll(live, shift, 0) if shift else live
+            convolved = convolved + taps_ref[tap : tap + 1, :] * moved[window:, :]
+        gates = right_half[:, wide:]
+        heads = (attended + gates * convolved).astype(jnp.bfloat16)
+        mixed[rows, :] = rows_dot(heads, spread_one).astype(jnp.bfloat16)
+
+    block_total = row_total // block_rows
+    pl.loop(0, block_total // 2)(attend)
+    tick(ffn_phase, 1)
+    pl.loop(block_total // 2, block_total)(attend)
+
+    for part, rows_ref in ((0, key_rows), (1, value_rows)):
+        tail = jnp.dot(
+            slot_back,
+            rows_ref[row_total : row_total + window, :],
+            preferred_element_type=jnp.float32,
+        )
+        renewed_ref[part] = rows_dot(tail.astype(jnp.bfloat16), spread_one).astype(jnp.bfloat16)
+
+    for distance in range(1, group_size):
+        gather_copy(normed_all, gather_send, gather_recv, distance).wait_send()
+    for distance in list(range(1, group_size)) + [0]:
+        rows = group_rows(peer(distance))
+        normed_all[rows, :] = rows_dot(mixed[rows, :], out_all[...]).astype(jnp.bfloat16)
+        if distance:
+            attn_copy(distance).start()
+
+    ticks(ffn_phase, 2, min(5, last + 1))
+    attn_sum = normed_all[group_rows(my_tp), :].astype(jnp.float32)
+    for distance in range(1, group_size):
+        attn_copy(distance).wait_recv()
+        attn_sum = attn_sum + attn_got[distance - 1].astype(jnp.float32)
+    residual = (tokens_ref[...].astype(jnp.float32) + attn_sum).astype(jnp.bfloat16)
+    residual_ref[...] = residual
+    ffn_in_all[group_rows(my_tp), :] = normed(residual, ffn_gain_ref[...])
+    for distance in range(1, group_size):
+        gather_copy(ffn_in_all, ffn_send, ffn_recv, distance).start()
+
+    ticks(ffn_phase, min(5, last + 1), last + 1)
+    begin(down_phase)
+    for distance in range(1, group_size):
+        gather_arrived(ffn_in_all, ffn_send, ffn_recv, distance)
+    own_copy(2).wait()
+    own_copy(3).wait()
+    finish(ffn_phase)
+
+    tile_count = hidden // 256
+    early = 1 + tile_count // 3
+
+    @pl.loop(0, tile_count)
+    def _(tile):
+        begin_col = pl.multiple_of(tile * 256, 256)
+        gate = jnp.dot(
+            ffn_in_all[...], ffn_all[:, pl.ds(begin_col, 256)], preferred_element_type=jnp.float32
+        )
+        up = jnp.dot(
+            ffn_in_all[...],
+            ffn_all[:, pl.ds(pl.multiple_of(hidden + begin_col, 256), 256)],
+            preferred_element_type=jnp.float32,
+        )
+        activated = gate / (1.0 + jnp.exp(-gate)) * up
+        shared[:, pl.ds(begin_col, 256)] = activated.astype(jnp.bfloat16)
+
+        @pl.when(tile % 3 == 2)
+        def _():
+            tick(down_phase, tile // 3 + 1)
+
+    def consume(step):
+        for direction in range(2):
+            block = shard_req(direction, step) * 2 + direction
+            down_part[block] = rows_dot(
+                shared[...], down_all[pl.ds(half_begin(direction, step), half), :]
+            ).astype(jnp.bfloat16)
+            for distance in range(1, group_size):
+                down_copy(distance, direction, step).start()
+
+    pl.loop(0, early)(consume)
+
+    @pl.loop(early, last + 1)
+    def _(step):
+        tick(down_phase, step)
+        consume(step)
+
+    finish(down_phase)
+    consume(ring_size - 1)
+
+    @pl.loop(0, ring_size)
+    def _(step):
+        for direction in range(2):
+            block = shard_req(direction, step) * 2 + direction
+            total = down_part[block, group_rows(my_tp), :].astype(jnp.float32)
+            for distance in range(1, group_size):
+                down_copy(distance, direction, step).wait_recv()
+                total = total + down_got[distance - 1, block].astype(jnp.float32)
+            ffn_sum_ref[block] = total
+
+    for stream in range(len(streams)):
+        for direction in range(2):
+            ring_copy(stream, direction, 0, True).wait_send()
+
+            @pl.loop(1, last + 1)
+            def _(step):
+                ring_copy(stream, direction, step, False).wait_send()
+
+    for distance in range(1, group_size):
+        attn_copy(distance).wait_send()
+        gather_copy(ffn_in_all, ffn_send, ffn_recv, distance).wait_send()
+
+        @pl.loop(0, ring_size)
+        def _(step):
+            for direction in range(2):
+                down_copy(distance, direction, step).wait_send()
+
+
+def fused(
+    ring_size,
+    group_size,
+    tokens,
+    norm_gain,
+    ffn_gain,
+    mix_weight,
+    out_weight,
+    ffn_weight,
+    down_weight,
+    conv_taps,
+    past_cache,
+    cached_len,
+):
+    own_rows, width = tokens.shape
+    row_total = own_rows * group_size
+    shard_rows, _, feat_width = mix_weight.shape
+    hidden = ffn_weight.shape[2]
+    half = shard_rows // 2
+    head_count = feat_width // HD
+    wide = head_count * 128
+    window = past_cache.shape[2]
+
+    def widen(array):
+        heads = array.reshape(array.shape[0], head_count, HD)
+        return jnp.pad(heads, ((0, 0), (0, 0), (0, 128 - HD))).reshape(array.shape[0], wide)
+
+    spread_table = np.zeros((2, feat_width, 2, head_count, 128), np.float32)
+    for part in range(2):
+        for feature in range(feat_width):
+            spread_table[part, feature, part, feature // HD, feature % HD] = 1.0
+    spread = jnp.asarray(spread_table.reshape(2 * feat_width, 2 * wide), jnp.bfloat16)
+    bf16, f32 = jnp.bfloat16, jnp.float32
+    in_vmem = pl.BlockSpec(memory_space=pltpu.VMEM)
+    in_place = pl.BlockSpec(memory_space=pl.ANY)
+    peers = group_size - 1
+    ring_sems = pltpu.SemaphoreType.DMA((7 * 2 * (ring_size - 1),))
+    peer_sems = pltpu.SemaphoreType.DMA((peers,))
+    down_sems = pltpu.SemaphoreType.DMA((peers * 2 * ring_size,))
+    ffn_sum, residual, renewed = pl.pallas_call(
+        functools.partial(layer_kernel, ring_size, group_size, window, head_count, HD),
+        out_shape=(
+            jax.ShapeDtypeStruct((2 * ring_size, own_rows, half), f32),
+            jax.ShapeDtypeStruct((own_rows, width), bf16),
+            jax.ShapeDtypeStruct((2, window, feat_width), bf16),
+        ),
+        in_specs=[in_vmem] * 5
+        + [pl.BlockSpec(memory_space=pltpu.SMEM)]
+        + [in_vmem]
+        + [in_place] * 4,
+        out_specs=(in_vmem,) * 3,
+        scratch_shapes=[
+            pltpu.VMEM((width, 4 * feat_width), bf16),
+            pltpu.VMEM((width, feat_width), bf16),
+            pltpu.VMEM((width, 2 * hidden), bf16),
+            pltpu.VMEM((width, hidden), bf16),
+            pltpu.VMEM((row_total, width), bf16),
+            pltpu.VMEM((row_total, width), bf16),
+            pltpu.VMEM((window + row_total, wide), bf16),
+            pltpu.VMEM((window + row_total, wide), bf16),
+            pltpu.VMEM((row_total, feat_width), bf16),
+            pltpu.VMEM((peers, own_rows, width), bf16),
+            pltpu.VMEM((row_total, hidden), bf16),
+            pltpu.VMEM((2 * ring_size, row_total, half), bf16),
+            pltpu.VMEM((peers, 2 * ring_size, own_rows, half), bf16),
+            ring_sems,
+            ring_sems,
+            pltpu.SemaphoreType.DMA((4,)),
+            peer_sems,
+            peer_sems,
+            peer_sems,
+            peer_sems,
+            peer_sems,
+            peer_sems,
+            down_sems,
+            down_sems,
+        ],
+        compiler_params=pltpu.CompilerParams(
+            collective_id=0, has_side_effects=True, vmem_limit_bytes=63 * 1024 * 1024
+        ),
+    )(
+        tokens,
+        norm_gain.reshape(1, width),
+        ffn_gain.reshape(1, width),
+        widen(conv_taps),
+        past_cache[0],
+        cached_len,
+        spread,
+        mix_weight.reshape(shard_rows, 4 * feat_width),
+        out_weight.T,
+        ffn_weight.reshape(shard_rows, 2 * hidden),
+        down_weight.T,
+    )
+    ffn_part = jnp.transpose(ffn_sum, (1, 0, 2)).reshape(own_rows, width)
+    layer_out = (residual.astype(f32) + ffn_part).astype(bf16)
+    return (layer_out, renewed[None])
+
 
 def solution(mesh):
     in_specs = (
@@ -135,4 +648,25 @@
         P("req"),
     )
     out_specs = (P(("req", "tp"), None), P("req", None, None, "tp"))
-    return jax.shard_map(local, mesh=mesh, in_specs=in_specs, out_specs=out_specs, check_vma=False)
+    ring_size, group_size = mesh.shape["req"], mesh.shape["tp"]
+
+    def device_layer(*args):
+        tokens, mix_weight, ffn_weight = args[0], args[3], args[5]
+        shard_rows, _, feat_width = mix_weight.shape
+        fits = (
+            ring_size > 5
+            and ring_size % 2 == 0
+            and group_size == 4
+            and shard_rows % 32 == 0
+            and feat_width % (HD * 4) == 0
+            and feat_width * 4 == ffn_weight.shape[2]
+            and ffn_weight.shape[2] % 256 == 0
+            and tokens.shape[0] == 256
+        )
+        if fits:
+            return fused(ring_size, group_size, *args)
+        return local(*args)
+
+    return jax.shard_map(
+        device_layer, mesh=mesh, in_specs=in_specs, out_specs=out_specs, check_vma=False
+    )

time: 671 us -> 305 us (0.45)
  waiting for transfers between devices: 469 us -> 0 us
  Pallas kernels: 0 us -> 286 us
  local copies, waits for them, and re-layouts: 92.8 us -> 15.4 us
  matrix products: 63 us -> 0 us
  other arithmetic: 24.3 us -> 1.08 us
  between operations: 15 us -> 1.44 us
    all_gather x6 -> x0, waiting for transfers between devices: 408 us -> none  [the longest x1 178 us: local(): lax.all_gather(ffn_weight, 'req', axis=0, tiled=True)]
    pallas_call x0 -> x1, Pallas kernels: none -> 286 us  [fused(): pl.pallas_call(functools.partial(layer_kernel, ring_size, group_size, win...]
    dot_general x8 -> x0, matrix products: 63 us -> none  [the longest x2 32.2 us: add_rows(): jnp.dot(left, shard_piece.reshape(shard_piece.shape[0], -1), preferred_el...]
    reduce_scatter x2 -> x0, waiting for transfers between devices: 59.6 us -> none  [the longest x1 40.3 us: local(): lax.psum_scatter(jnp.dot(mixed_heads, out_columns, preferred_element_type...]
    dynamic_update_slice x4 -> x0, local copies, waits for them, and re-layouts: 36.4 us -> none  [window_attend(): lax.map(one_block, jnp.arange(row_count // block_rows, dtype=jnp.int32))]
    another operation x3 -> x0, local copies, waits for them, and re-layouts: 14.6 us -> none  [mix_request(): renewed = jnp.stack([projected[:, 1], projected[:, 2]])[:, slot_source]]
    unnamed x19 -> x11, local copies, waits for them, and re-layouts: 17.6 us -> 4.38 us
    all_gather x1 -> x0, local copies, waits for them, and re-layouts: 12.9 us -> none  [local(): lax.all_gather(mix_weight, 'req', axis=0, tiled=True)]
  transfers between devices with their start and end apart: 8 -> 0, of which waited for: 7 -> 0; matrix products, arithmetic and copies ran while one was open for 23% -> 0% of each run, Pallas kernels for 0% -> 0%
where the time goes in v1:
time: 305 us; the launch traced here: 304 us
  Pallas kernels  286 us (94%)
  local copies, waits for them, and re-layouts  15.4 us (5%)
    pallas_call x1, Pallas kernels, fused(): pl.pallas_call(functools.partial(layer_kernel, ring_size, group_size, win...  286 us

profile of v1, /device:TPU:1, one launch (start us, length us, event | category | flops | bytes accessed | tf_op | source)
XLA Modules:
  0.0 304.3 jit_solution(17578232053489295264)
XLA Ops:
  0.6 0.0 copy-start
  1.4 0.8 reshape.27
  2.2 0.6 copy.21
  2.8 1.3 reshape.25.norm_gain_ref
  4.1 1.3 reshape.26.ffn_gain_ref
  5.4 1.8 copy.15
  7.1 3.0 reshape.29.mix_ref
  10.1 0.0 copy-done
  10.1 1.3 copy.19
  11.5 286.3 %shard_map.122 = (f32[16,256,112]{2,1,0:T(8,128)}, bf16[256,1792]{1,0:T(8,128)(2,1)}, bf16[2,64,448]{2,1,0:T(8,128)(2,1)}) custom-call(bf16[256,1792]{1,0:T(8,128)(2,1)} %tokens_ref.1, f32[1,1792]{1,0:T(1,128)} %reshape.25.norm_gain_ref, f32[1,1792]{1,0:T(1,128)} %reshape.26.ffn_gain_ref, f32[3,512]{1,0:T(4,128)} %bitcast.21, bf16[2,64,448]{2,1,0:T(8,128)(2,1)} %bitcast.19, ...), custom_call_target="tpu_custom_call" | custom-call | tf_op jit(solution)/shard_map/pallas_call | solution.py:578
  297.8 2.8 copy.16
  300.6 0.0 copy-start.1
  300.6 1.9 copy.17
  302.5 0.0 copy-done.1
  302.5 0.0 copy-start.2
  302.6 1.1 add_convert_fusion
  303.6 0.0 copy-done.2
  303.6 0.7 copy.24
  (1 shorter events, 0.0 us)
Async XLA Ops:
  0.6 9.5 %copy-start = (bf16[224,2,1792]{2,1,0:T(2,128)(2,1)S(1)}, bf16[224,2,1792]{2,1,0:T(2,128)(2,1)}, u32[]{:S(2)}) copy-start(bf16[224,2,1792]{2,1,0:T(2,128)(2,1)} %param.16) | copy-start | bytes 4816900
  300.6 1.9 copy-start.1
  302.5 1.1 copy-start.2

commit v2 on v1

--- a/solution.py
+++ b/solution.py
@@ -196,16 +196,22 @@
     wide = head_count * 128
     last = ring_size - 2
 
+    tile_count = hidden // 256
+    early_tiles = (tile_count + 1) // 2
+    early_hidden = early_tiles * 256
+
     streams = [
         (out_ref, out_all, 0, feat_width),
         (mix_ref, mix_all, 0, half_cols),
         (mix_ref, mix_all, half_cols, half_cols),
-        (ffn_ref, ffn_all, 0, hidden),
-        (ffn_ref, ffn_all, hidden, hidden),
+        (ffn_ref, ffn_all, 0, early_hidden),
+        (ffn_ref, ffn_all, hidden, early_hidden),
+        (ffn_ref, ffn_all, early_hidden, hidden - early_hidden),
+        (ffn_ref, ffn_all, hidden + early_hidden, hidden - early_hidden),
         (down_ref, down_all, 0, hidden // 2),
         (down_ref, down_all, hidden // 2, hidden // 2),
     ]
-    mix_phase, ffn_phase, down_phase = (0, 1, 2), (3, 4), (5, 6)
+    mix_phase, early_phase, late_phase, down_phase = (0, 1, 2), (3, 4), (5, 6), (7, 8)
 
     def shard_req(direction, step):
         if direction == 0:
@@ -278,36 +284,32 @@
     def group_rows(member):
         return pl.ds(pl.multiple_of(member * own_rows, 16), own_rows)
 
-    def gather_copy(whole, sends, recvs, distance):
-        rows = whole.at[group_rows(my_tp)]
+    sibling = my_tp + 1 - 2 * (my_tp % 2)
+    across = peer(2)
+    diagonal = (sibling + 2) % group_size
+
+    def peer_copy(source, target, sends, recvs, index, member):
         return pltpu.make_async_remote_copy(
-            src_ref=rows,
-            dst_ref=rows,
-            send_sem=sends.at[distance - 1],
-            recv_sem=recvs.at[distance - 1],
-            device_id={"tp": peer(distance)},
+            src_ref=source,
+            dst_ref=target,
+            send_sem=sends.at[index],
+            recv_sem=recvs.at[index],
+            device_id={"tp": member},
             device_id_type=MESH,
         )
 
-    def gather_arrived(whole, sends, recvs, distance):
-        rows = whole.at[group_rows((my_tp + group_size - distance) % group_size)]
-        pltpu.make_async_remote_copy(
-            src_ref=rows,
-            dst_ref=rows,
-            send_sem=sends.at[distance - 1],
-            recv_sem=recvs.at[distance - 1],
-            device_id={"tp": peer(distance)},
-            device_id_type=MESH,
-        ).wait_recv()
-
-    def attn_copy(distance):
-        return pltpu.make_async_remote_copy(
-            src_ref=normed_all.at[group_rows(peer(distance))],
-            dst_ref=attn_got.at[distance - 1],
-            send_sem=attn_send.at[distance - 1],
-            recv_sem=attn_recv.at[distance - 1],
-            device_id={"tp": peer(distance)},
-            device_id_type=MESH,
+    def gather_copy(whole, sends, recvs, index):
+        rows = whole.at[group_rows(across if index == 2 else my_tp)]
+        return peer_copy(rows, rows, sends, recvs, index, sibling if index else across)
+
+    def gather_arrived(whole, sends, recvs, index):
+        rows = whole.at[group_rows((across, sibling, diagonal)[index])]
+        peer_copy(rows, rows, sends, recvs, index, sibling if index else across).wait_recv()
+
+    def attn_copy(index):
+        rows = normed_all.at[group_rows((sibling, diagonal, across)[index])]
+        return peer_copy(
+            rows, attn_got.at[index], attn_send, attn_recv, index, across if index == 2 else sibling
         )
 
     def down_copy(distance, direction, step):
@@ -342,8 +344,8 @@
     for index in range(4):
         own_copy(index).start()
     normed_all[group_rows(my_tp), :] = normed(tokens_ref[...], norm_gain_ref[...])
-    for distance in range(1, group_size):
-        gather_copy(normed_all, gather_send, gather_recv, distance).start()
+    for index in range(2):
+        gather_copy(normed_all, gather_send, gather_recv, index).start()
 
     length = length_ref[0]
     row_ids = lax.broadcasted_iota(jnp.int32, (window, window), 0)
@@ -359,10 +361,13 @@
             earlier.astype(jnp.bfloat16), spread_one, preferred_element_type=jnp.float32
         ).astype(jnp.bfloat16)
 
-    ticks(mix_phase, 1, last + 1)
-    begin(ffn_phase)
-    for distance in range(1, group_size):
-        gather_arrived(normed_all, gather_send, gather_recv, distance)
+    ticks(mix_phase, 1, 4)
+    gather_arrived(normed_all, gather_send, gather_recv, 0)
+    gather_copy(normed_all, gather_send, gather_recv, 2).start()
+    ticks(mix_phase, 4, last + 1)
+    begin(early_phase)
+    for index in (1, 2):
+        gather_arrived(normed_all, gather_send, gather_recv, index)
     own_copy(0).wait()
     own_copy(1).wait()
     finish(mix_phase)
@@ -429,9 +434,15 @@
         mixed[rows, :] = rows_dot(heads, spread_one).astype(jnp.bfloat16)
 
     block_total = row_total // block_rows
-    pl.loop(0, block_total // 2)(attend)
-    tick(ffn_phase, 1)
-    pl.loop(block_total // 2, block_total)(attend)
+    tick(early_phase, 1)
+
+    @pl.loop(0, block_total)
+    def _(block):
+        attend(block)
+
+        @pl.when(block % 3 == 2)
+        def _():
+            tick(early_phase, 2 + block // 3)
 
     for part, rows_ref in ((0, key_rows), (1, value_rows)):
         tail = jnp.dot(
@@ -441,38 +452,43 @@
         )
         renewed_ref[part] = rows_dot(tail.astype(jnp.bfloat16), spread_one).astype(jnp.bfloat16)
 
-    for distance in range(1, group_size):
-        gather_copy(normed_all, gather_send, gather_recv, distance).wait_send()
-    for distance in list(range(1, group_size)) + [0]:
-        rows = group_rows(peer(distance))
+    for index in range(3):
+        gather_copy(normed_all, gather_send, gather_recv, index).wait_send()
+    tick(early_phase, 4)
+    for index, member in enumerate((sibling, diagonal, across, my_tp)):
+        rows = group_rows(member)
         normed_all[rows, :] = rows_dot(mixed[rows, :], out_all[...]).astype(jnp.bfloat16)
-        if distance:
-            attn_copy(distance).start()
-
-    ticks(ffn_phase, 2, min(5, last + 1))
+        if index < 2:
+            attn_copy(index).start()
+    ticks(early_phase, 5, last)
+    attn_copy(1).wait_recv()
+    rows = group_rows(across)
+    normed_all[rows, :] = (
+        normed_all[rows, :].astype(jnp.float32) + attn_got[1].astype(jnp.float32)
+    ).astype(jnp.bfloat16)
+    attn_copy(2).start()
+    tick(early_phase, last)
+    begin(late_phase)
+    own_copy(2).wait()
+    own_copy(3).wait()
+    finish(early_phase)
     attn_sum = normed_all[group_rows(my_tp), :].astype(jnp.float32)
-    for distance in range(1, group_size):
-        attn_copy(distance).wait_recv()
-        attn_sum = attn_sum + attn_got[distance - 1].astype(jnp.float32)
+    for index in (0, 2):
+        attn_copy(index).wait_recv()
+        attn_sum = attn_sum + attn_got[index].astype(jnp.float32)
     residual = (tokens_ref[...].astype(jnp.float32) + attn_sum).astype(jnp.bfloat16)
     residual_ref[...] = residual
     ffn_in_all[group_rows(my_tp), :] = normed(residual, ffn_gain_ref[...])
-    for distance in range(1, group_size):
-        gather_copy(ffn_in_all, ffn_send, ffn_recv, distance).start()
-
-    ticks(ffn_phase, min(5, last + 1), last + 1)
-    begin(down_phase)
-    for distance in range(1, group_size):
-        gather_arrived(ffn_in_all, ffn_send, ffn_recv, distance)
-    own_copy(2).wait()
-    own_copy(3).wait()
-    finish(ffn_phase)
-
-    tile_count = hidden // 256
-    early = 1 + tile_count // 3
-
-    @pl.loop(0, tile_count)
-    def _(tile):
+    for index in range(2):
+        gather_copy(ffn_in_all, ffn_send, ffn_recv, index).start()
+
+    ticks(late_phase, 1, 4)
+    gather_arrived(ffn_in_all, ffn_send, ffn_recv, 0)
+    gather_copy(ffn_in_all, ffn_send, ffn_recv, 2).start()
+    for index in (1, 2):
+        gather_arrived(ffn_in_all, ffn_send, ffn_recv, index)
+
+    def activate(tile):
         begin_col = pl.multiple_of(tile * 256, 256)
         gate = jnp.dot(
             ffn_in_all[...], ffn_all[:, pl.ds(begin_col, 256)], preferred_element_type=jnp.float32
@@ -485,9 +501,25 @@
         activated = gate / (1.0 + jnp.exp(-gate)) * up
         shared[:, pl.ds(begin_col, 256)] = activated.astype(jnp.bfloat16)
 
-        @pl.when(tile % 3 == 2)
+    @pl.loop(0, early_tiles)
+    def _(tile):
+        activate(tile)
+
+        @pl.when(tile + 4 <= last)
         def _():
-            tick(down_phase, tile // 3 + 1)
+            tick(late_phase, tile + 4)
+
+    ticks(late_phase, 4 + early_tiles, last + 1)
+    begin(down_phase)
+    finish(late_phase)
+
+    @pl.loop(early_tiles, tile_count)
+    def _(tile):
+        activate(tile)
+
+        @pl.when(tile == early_tiles + 1)
+        def _():
+            tick(down_phase, 1)
 
     def consume(step):
         for direction in range(2):
@@ -498,9 +530,9 @@
             for distance in range(1, group_size):
                 down_copy(distance, direction, step).start()
 
-    pl.loop(0, early)(consume)
-
-    @pl.loop(early, last + 1)
+    pl.loop(0, 2)(consume)
+
+    @pl.loop(2, last + 1)
     def _(step):
         tick(down_phase, step)
         consume(step)
@@ -526,9 +558,10 @@
             def _(step):
                 ring_copy(stream, direction, step, False).wait_send()
 
+    for index in range(3):
+        attn_copy(index).wait_send()
+        gather_copy(ffn_in_all, ffn_send, ffn_recv, index).wait_send()
     for distance in range(1, group_size):
-        attn_copy(distance).wait_send()
-        gather_copy(ffn_in_all, ffn_send, ffn_recv, distance).wait_send()
 
         @pl.loop(0, ring_size)
         def _(step):
@@ -572,7 +605,7 @@
     in_vmem = pl.BlockSpec(memory_space=pltpu.VMEM)
     in_place = pl.BlockSpec(memory_space=pl.ANY)
     peers = group_size - 1
-    ring_sems = pltpu.SemaphoreType.DMA((7 * 2 * (ring_size - 1),))
+    ring_sems = pltpu.SemaphoreType.DMA((9 * 2 * (ring_size - 1),))
     peer_sems = pltpu.SemaphoreType.DMA((peers,))
     down_sems = pltpu.SemaphoreType.DMA((peers * 2 * ring_size,))
     ffn_sum, residual, renewed = pl.pallas_call(
@@ -654,12 +687,13 @@
         tokens, mix_weight, ffn_weight = args[0], args[3], args[5]
         shard_rows, _, feat_width = mix_weight.shape
         fits = (
-            ring_size > 5
-            and ring_size % 2 == 0
+            ring_size == 8
             and group_size == 4
             and shard_rows % 32 == 0
             and feat_width % (HD * 4) == 0
             and feat_width * 4 == ffn_weight.shape[2]
+            and tokens.shape[1] == 8 * shard_rows
+            and ffn_weight.shape[2] >= 1024
             and ffn_weight.shape[2] % 256 == 0
             and tokens.shape[0] == 256
         )

time: 305 us -> 304 us (level)
  no operation moved by 1% of the time
where the time goes in v2:
time: 304 us
  Pallas kernels  286 us (94%)
  local copies, waits for them, and re-layouts  15.4 us (5%)
    pallas_call x1, Pallas kernels, fused(): pl.pallas_call(functools.partial(layer_kernel, ring_size, group_size, win...  286 us

profile of v2, /device:TPU:1, one launch (start us, length us, event | category | flops | bytes accessed | tf_op | source)
XLA Modules:
  0.0 303.6 jit_solution(5103443059594717314)
XLA Ops:
  0.6 0.0 copy-start
  1.4 0.8 reshape.27
  2.2 0.6 copy.21
  2.8 1.3 reshape.25.norm_gain_ref
  4.1 1.3 reshape.26.ffn_gain_ref
  5.4 1.8 copy.15
  7.1 3.0 reshape.29.mix_ref
  10.1 0.0 copy-done
  10.1 1.3 copy.19
  11.5 285.6 %shard_map.122 = (f32[16,256,112]{2,1,0:T(8,128)}, bf16[256,1792]{1,0:T(8,128)(2,1)}, bf16[2,64,448]{2,1,0:T(8,128)(2,1)}) custom-call(bf16[256,1792]{1,0:T(8,128)(2,1)} %tokens_ref.1, f32[1,1792]{1,0:T(1,128)} %reshape.25.norm_gain_ref, f32[1,1792]{1,0:T(1,128)} %reshape.26.ffn_gain_ref, f32[3,512]{1,0:T(4,128)} %bitcast.21, bf16[2,64,448]{2,1,0:T(8,128)(2,1)} %bitcast.19, ...), custom_call_target="tpu_custom_call" | custom-call | tf_op jit(solution)/shard_map/pallas_call | solution.py:611
  297.1 2.8 copy.16
  299.9 0.0 copy-start.1
  299.9 1.9 copy.17
  301.8 0.0 copy-done.1
  301.9 0.0 copy-start.2
  301.9 1.1 add_convert_fusion
  302.9 0.0 copy-done.2
  302.9 0.7 copy.24
  (1 shorter events, 0.0 us)
Async XLA Ops:
  0.6 9.5 %copy-start = (bf16[224,2,1792]{2,1,0:T(2,128)(2,1)S(1)}, bf16[224,2,1792]{2,1,0:T(2,128)(2,1)}, u32[]{:S(2)}) copy-start(bf16[224,2,1792]{2,1,0:T(2,128)(2,1)} %param.16) | copy-start | bytes 4816900
  299.9 1.9 copy-start.1
  301.9 1.1 copy-start.2

commit v3 on v2

--- a/solution.py
+++ b/solution.py
@@ -154,8 +154,7 @@
     out_ref,
     ffn_ref,
     down_ref,
-    ffn_sum_ref,
-    residual_ref,
+    layer_out_ref,
     renewed_ref,
     mix_all,
     out_all,
@@ -170,6 +169,8 @@
     shared,
     down_part,
     down_got,
+    ffn_sum,
+    residual_own,
     ring_send,
     ring_recv,
     own_sem,
@@ -211,7 +212,12 @@
         (down_ref, down_all, 0, hidden // 2),
         (down_ref, down_all, hidden // 2, hidden // 2),
     ]
-    mix_phase, early_phase, late_phase, down_phase = (0, 1, 2), (3, 4), (5, 6), (7, 8)
+    mix_phase, early_phase, late_phase, down_phase = (
+        ((1,), (2, 0)),
+        ((3,), (4,)),
+        ((5,), (6,)),
+        ((7,), (8,)),
+    )
 
     def shard_req(direction, step):
         if direction == 0:
@@ -250,13 +256,13 @@
             device_id_type=MESH,
         ).wait_recv()
 
-    def begin(phase):
-        for stream in phase:
+    def begin(lane):
+        for stream in lane:
             for direction in range(2):
                 ring_copy(stream, direction, 0, True).start()
 
-    def tick(phase, step):
-        for stream in phase:
+    def tick(lane, step):
+        for stream in lane:
             for direction in range(2):
                 ring_arrived(stream, direction, step - 1)
                 ring_copy(stream, direction, step, False).start()
@@ -264,12 +270,19 @@
     def ticks(phase, low, high):
         @pl.loop(low, high)
         def _(step):
-            tick(phase, step)
+            for lane in phase:
+                tick(lane, step)
+
+    def turn(phase, following):
+        for lane, next_lane in zip(phase, following):
+            tick(lane, last)
+            begin(next_lane)
 
     def finish(phase):
-        for stream in phase:
-            for direction in range(2):
-                ring_arrived(stream, direction, last)
+        for lane in phase:
+            for stream in lane:
+                for direction in range(2):
+                    ring_arrived(stream, direction, last)
 
     def own_copy(index):
         source, whole = ((mix_ref, mix_all), (out_ref, out_all), (ffn_ref, ffn_all), (down_ref, down_all))[index]
@@ -340,10 +353,11 @@
         )
     pl.semaphore_wait(barrier, 1 + group_size)
 
-    begin(mix_phase)
+    begin(mix_phase[0])
+    normed_all[group_rows(my_tp), :] = normed(tokens_ref[...], norm_gain_ref[...])
+    begin(mix_phase[1])
     for index in range(4):
         own_copy(index).start()
-    normed_all[group_rows(my_tp), :] = normed(tokens_ref[...], norm_gain_ref[...])
     for index in range(2):
         gather_copy(normed_all, gather_send, gather_recv, index).start()
 
@@ -364,8 +378,8 @@
     ticks(mix_phase, 1, 4)
     gather_arrived(normed_all, gather_send, gather_recv, 0)
     gather_copy(normed_all, gather_send, gather_recv, 2).start()
-    ticks(mix_phase, 4, last + 1)
-    begin(early_phase)
+    ticks(mix_phase, 4, last)
+    turn(mix_phase, early_phase)
     for index in (1, 2):
         gather_arrived(normed_all, gather_send, gather_recv, index)
     own_copy(0).wait()
@@ -378,6 +392,10 @@
         shared[:, cols] = jnp.dot(
             normed_all[...], mix_all[:, cols], preferred_element_type=jnp.float32
         ).astype(jnp.bfloat16)
+
+        @pl.when(tile == 3)
+        def _():
+            tick(early_phase[0], 1)
 
     block_rows = 128
     key_count = block_rows + window
@@ -434,15 +452,17 @@
         mixed[rows, :] = rows_dot(heads, spread_one).astype(jnp.bfloat16)
 
     block_total = row_total // block_rows
-    tick(early_phase, 1)
+    tick(early_phase[1], 1)
 
     @pl.loop(0, block_total)
     def _(block):
         attend(block)
 
-        @pl.when(block % 3 == 2)
-        def _():
-            tick(early_phase, 2 + block // 3)
+        for side in range(2):
+
+            @pl.when(block % 3 == 1 + side)
+            def _():
+                tick(early_phase[side], 2 + block // 3)
 
     for part, rows_ref in ((0, key_rows), (1, value_rows)):
         tail = jnp.dot(
@@ -454,21 +474,22 @@
 
     for index in range(3):
         gather_copy(normed_all, gather_send, gather_recv, index).wait_send()
-    tick(early_phase, 4)
+    tick(early_phase[1], 4)
     for index, member in enumerate((sibling, diagonal, across, my_tp)):
         rows = group_rows(member)
         normed_all[rows, :] = rows_dot(mixed[rows, :], out_all[...]).astype(jnp.bfloat16)
         if index < 2:
             attn_copy(index).start()
-    ticks(early_phase, 5, last)
+        if index == 1:
+            tick(early_phase[0], 5)
+    tick(early_phase[1], 5)
     attn_copy(1).wait_recv()
     rows = group_rows(across)
     normed_all[rows, :] = (
         normed_all[rows, :].astype(jnp.float32) + attn_got[1].astype(jnp.float32)
     ).astype(jnp.bfloat16)
     attn_copy(2).start()
-    tick(early_phase, last)
-    begin(late_phase)
+    turn(early_phase, late_phase)
     own_copy(2).wait()
     own_copy(3).wait()
     finish(early_phase)
@@ -477,7 +498,7 @@
         attn_copy(index).wait_recv()
         attn_sum = attn_sum + attn_got[index].astype(jnp.float32)
     residual = (tokens_ref[...].astype(jnp.float32) + attn_sum).astype(jnp.bfloat16)
-    residual_ref[...] = residual
+    residual_own[...] = residual
     ffn_in_all[group_rows(my_tp), :] = normed(residual, ffn_gain_ref[...])
     for index in range(2):
         gather_copy(ffn_in_all, ffn_send, ffn_recv, index).start()
@@ -505,24 +526,29 @@
     def _(tile):
         activate(tile)
 
-        @pl.when(tile + 4 <= last)
-        def _():
-            tick(late_phase, tile + 4)
-
-    ticks(late_phase, 4 + early_tiles, last + 1)
-    begin(down_phase)
+        for side in range(2):
+
+            @pl.when(tile % 2 == side)
+            def _():
+                tick(late_phase[side], 4 + tile // 2)
+
+    turn(late_phase, down_phase)
     finish(late_phase)
 
     @pl.loop(early_tiles, tile_count)
     def _(tile):
         activate(tile)
 
+        @pl.when(tile == early_tiles)
+        def _():
+            tick(down_phase[0], 1)
+
         @pl.when(tile == early_tiles + 1)
         def _():
-            tick(down_phase, 1)
-
-    def consume(step):
-        for direction in range(2):
+            tick(down_phase[1], 1)
+
+    def consume(step, directions=(0, 1)):
+        for direction in directions:
             block = shard_req(direction, step) * 2 + direction
             down_part[block] = rows_dot(
                 shared[...], down_all[pl.ds(half_begin(direction, step), half), :]
@@ -530,13 +556,18 @@
             for distance in range(1, group_size):
                 down_copy(distance, direction, step).start()
 
-    pl.loop(0, 2)(consume)
-
-    @pl.loop(2, last + 1)
+    tick(down_phase[0], 2)
+    consume(0)
+    tick(down_phase[1], 2)
+    consume(1)
+
+    @pl.loop(3, last + 1)
     def _(step):
-        tick(down_phase, step)
-        consume(step)
-
+        for side in range(2):
+            tick(down_phase[side], step)
+            consume(step - 1, (side,))
+
+    consume(last)
     finish(down_phase)
     consume(ring_size - 1)
 
@@ -548,7 +579,16 @@
             for distance in range(1, group_size):
                 down_copy(distance, direction, step).wait_recv()
                 total = total + down_got[distance - 1, block].astype(jnp.float32)
-            ffn_sum_ref[block] = total
+            ffn_sum[block] = total
+
+    for part in range(2):
+        rows = slice(part * (own_rows // 2), (part + 1) * (own_rows // 2))
+        ffn_part = jnp.concatenate(
+            [ffn_sum[block, rows, :] for block in range(2 * ring_size)], axis=1
+        )
+        layer_out_ref[rows, :] = (
+            residual_own[rows, :].astype(jnp.float32) + ffn_part
+        ).astype(jnp.bfloat16)
 
     for stream in range(len(streams)):
         for direction in range(2):
@@ -608,10 +648,9 @@
     ring_sems = pltpu.SemaphoreType.DMA((9 * 2 * (ring_size - 1),))
     peer_sems = pltpu.SemaphoreType.DMA((peers,))
     down_sems = pltpu.SemaphoreType.DMA((peers * 2 * ring_size,))
-    ffn_sum, residual, renewed = pl.pallas_call(
+    layer_out, renewed = pl.pallas_call(
         functools.partial(layer_kernel, ring_size, group_size, window, head_count, HD),
         out_shape=(
-            jax.ShapeDtypeStruct((2 * ring_size, own_rows, half), f32),
             jax.ShapeDtypeStruct((own_rows, width), bf16),
             jax.ShapeDtypeStruct((2, window, feat_width), bf16),
         ),
@@ -619,7 +658,7 @@
         + [pl.BlockSpec(memory_space=pltpu.SMEM)]
         + [in_vmem]
         + [in_place] * 4,
-        out_specs=(in_vmem,) * 3,
+        out_specs=(in_vmem,) * 2,
         scratch_shapes=[
             pltpu.VMEM((width, 4 * feat_width), bf16),
             pltpu.VMEM((width, feat_width), bf16),
@@ -634,6 +673,8 @@
             pltpu.VMEM((row_total, hidden), bf16),
             pltpu.VMEM((2 * ring_size, row_total, half), bf16),
             pltpu.VMEM((peers, 2 * ring_size, own_rows, half), bf16),
+            pltpu.VMEM((2 * ring_size, own_rows, half), f32),
+            pltpu.VMEM((own_rows, width), bf16),
             ring_sems,
             ring_sems,
             pltpu.SemaphoreType.DMA((4,)),
@@ -662,8 +703,6 @@
         ffn_weight.reshape(shard_rows, 2 * hidden),
         down_weight.T,
     )
-    ffn_part = jnp.transpose(ffn_sum, (1, 0, 2)).reshape(own_rows, width)
-    layer_out = (residual.astype(f32) + ffn_part).astype(bf16)
     return (layer_out, renewed[None])
 
 
@@ -693,8 +732,7 @@
             and feat_width % (HD * 4) == 0
             and feat_width * 4 == ffn_weight.shape[2]
             and tokens.shape[1] == 8 * shard_rows
-            and ffn_weight.shape[2] >= 1024
-            and ffn_weight.shape[2] % 256 == 0
+            and ffn_weight.shape[2] == 7 * 256
             and tokens.shape[0] == 256
         )
         if fits:

time: 304 us -> 297 us (0.977)
  Pallas kernels: 286 us -> 282 us
    pallas_call x1, Pallas kernels: 286 us -> 282 us  [fused(): pl.pallas_call(functools.partial(layer_kernel, ring_size, group_size, win...]
    unnamed x11 -> x10, local copies, waits for them, and re-layouts: 4.38 us -> 6.57 us
where the time goes in v3:
time: 297 us
  Pallas kernels  282 us (95%)
  local copies, waits for them, and re-layouts  12.9 us (4%)
    pallas_call x1, Pallas kernels, fused(): pl.pallas_call(functools.partial(layer_kernel, ring_size, group_size, win...  282 us
    unnamed x10, local copies, waits for them, and re-layouts  6.57 us

profile of v3, /device:TPU:1, one launch (start us, length us, event | category | flops | bytes accessed | tf_op | source)
XLA Modules:
  0.0 296.6 jit_solution(12008355540060365542)
XLA Ops:
  0.6 0.0 copy-start
  1.4 0.8 reshape.24
  2.2 0.6 copy.17
  2.8 1.3 reshape.22.norm_gain_ref
  4.1 1.3 reshape.23.ffn_gain_ref
  5.4 1.8 copy.13
  7.1 3.0 %reshape.26.mix_ref = bf16[224,1792]{1,0:T(8,128)(2,1)} reshape(bf16[224,4,448]{2,1,0:T(4,128)(2,1)} %param.14) | data formatting | bytes 1605632 | tf_op jit(solution)/shard_map/reshape | solution.py:701
  10.1 0.0 copy-done
  10.1 1.3 copy.15
  11.5 282.3 %shard_map.122 = (bf16[256,1792]{1,0:T(8,128)(2,1)}, bf16[2,64,448]{2,1,0:T(8,128)(2,1)}) custom-call(bf16[256,1792]{1,0:T(8,128)(2,1)} %tokens_ref.1, f32[1,1792]{1,0:T(1,128)} %reshape.22.norm_gain_ref, f32[1,1792]{1,0:T(1,128)} %reshape.23.ffn_gain_ref, f32[3,512]{1,0:T(4,128)} %bitcast.17, bf16[2,64,448]{2,1,0:T(8,128)(2,1)} %bitcast.15, ...), custom_call_target="tpu_custom_call" | custom-call | tf_op jit(solution)/shard_map/pallas_call | solution.py:651
  293.8 0.0 copy-start.1
  293.8 2.2 copy.21
  296.0 0.0 copy-done.1
  296.0 0.7 copy.22
  (1 shorter events, 0.0 us)
Async XLA Ops:
  0.6 9.5 %copy-start = (bf16[224,2,1792]{2,1,0:T(2,128)(2,1)S(1)}, bf16[224,2,1792]{2,1,0:T(2,128)(2,1)}, u32[]{:S(2)}) copy-start(bf16[224,2,1792]{2,1,0:T(2,128)(2,1)} %param.16) | copy-start | bytes 4816900
  293.8 2.2 copy-start.1

commit v4 on v3

--- a/solution.py
+++ b/solution.py
@@ -171,6 +171,7 @@
     down_got,
     ffn_sum,
     residual_own,
+    wide_taps,
     ring_send,
     ring_recv,
     own_sem,
@@ -354,7 +355,7 @@
     pl.semaphore_wait(barrier, 1 + group_size)
 
     begin(mix_phase[0])
-    normed_all[group_rows(my_tp), :] = normed(tokens_ref[...], norm_gain_ref[...])
+    normed_all[group_rows(my_tp), :] = normed(tokens_ref[...], norm_gain_ref[...].reshape(1, width))
     begin(mix_phase[1])
     for index in range(4):
         own_copy(index).start()
@@ -369,6 +370,13 @@
     slot_back = ((row_ids - col_ids - length - row_total) & (window - 1)) == 0
     slot_back = jnp.where(slot_back, 1.0, 0.0).astype(jnp.bfloat16)
     spread_one = spread_ref[0:feat_width, 0:wide]
+    taps = jnp.dot(
+        taps_ref[...],
+        spread_one.astype(jnp.float32),
+        precision=lax.Precision.HIGHEST,
+        preferred_element_type=jnp.float32,
+    )
+    wide_taps[...] = taps
     for part, rows_ref in ((0, key_rows), (1, value_rows)):
         earlier = jnp.dot(slot_order, cache_ref[part], preferred_element_type=jnp.float32)
         rows_ref[0:window, :] = jnp.dot(
@@ -446,7 +454,7 @@
         for tap in range(tap_count):
             shift = tap_count - 1 - tap
             moved = pltpu.roll(live, shift, 0) if shift else live
-            convolved = convolved + taps_ref[tap : tap + 1, :] * moved[window:, :]
+            convolved = convolved + wide_taps[tap : tap + 1, :] * moved[window:, :]
         gates = right_half[:, wide:]
         heads = (attended + gates * convolved).astype(jnp.bfloat16)
         mixed[rows, :] = rows_dot(heads, spread_one).astype(jnp.bfloat16)
@@ -499,7 +507,7 @@
         attn_sum = attn_sum + attn_got[index].astype(jnp.float32)
     residual = (tokens_ref[...].astype(jnp.float32) + attn_sum).astype(jnp.bfloat16)
     residual_own[...] = residual
-    ffn_in_all[group_rows(my_tp), :] = normed(residual, ffn_gain_ref[...])
+    ffn_in_all[group_rows(my_tp), :] = normed(residual, ffn_gain_ref[...].reshape(1, width))
     for index in range(2):
         gather_copy(ffn_in_all, ffn_send, ffn_recv, index).start()
 
@@ -631,10 +639,6 @@
     head_count = feat_width // HD
     wide = head_count * 128
     window = past_cache.shape[2]
-
-    def widen(array):
-        heads = array.reshape(array.shape[0], head_count, HD)
-        return jnp.pad(heads, ((0, 0), (0, 0), (0, 128 - HD))).reshape(array.shape[0], wide)
 
     spread_table = np.zeros((2, feat_width, 2, head_count, 128), np.float32)
     for part in range(2):
@@ -675,6 +679,7 @@
             pltpu.VMEM((peers, 2 * ring_size, own_rows, half), bf16),
             pltpu.VMEM((2 * ring_size, own_rows, half), f32),
             pltpu.VMEM((own_rows, width), bf16),
+            pltpu.VMEM((conv_taps.shape[0], wide), f32),
             ring_sems,
             ring_sems,
             pltpu.SemaphoreType.DMA((4,)),
@@ -692,9 +697,9 @@
         ),
     )(
         tokens,
-        norm_gain.reshape(1, width),
-        ffn_gain.reshape(1, width),
-        widen(conv_taps),
+        norm_gain,
+        ffn_gain,
+        conv_taps,
         past_cache[0],
         cached_len,
         spread,

time: 297 us -> 293 us (0.987)
  local copies, waits for them, and re-layouts: 12.9 us -> 8.94 us
    reshape x3 -> x0, local copies, waits for them, and re-layouts: 3.37 us -> none  [the longest x1 1.3 us: fused(): ffn_gain.reshape(1, width)]
    unnamed x10 -> x8, local copies, waits for them, and re-layouts: 6.57 us -> 5.96 us
where the time goes in v4:
time: 293 us
  Pallas kernels  282 us (96%)
  local copies, waits for them, and re-layouts  8.94 us (3%)
    pallas_call x1, Pallas kernels, fused(): pl.pallas_call(functools.partial(layer_kernel, ring_size, group_size, win...  282 us
    unnamed x8, local copies, waits for them, and re-layouts  5.96 us

profile of v4, /device:TPU:1, one launch (start us, length us, event | category | flops | bytes accessed | tf_op | source)
XLA Modules:
  0.0 292.7 jit_solution(13150526557459011625)
XLA Ops:
  0.6 0.0 copy-start
  1.4 1.8 copy.13
  3.2 3.0 %reshape.10.mix_ref = bf16[224,1792]{1,0:T(8,128)(2,1)} reshape(bf16[224,4,448]{2,1,0:T(4,128)(2,1)} %param.14) | data formatting | bytes 1605632 | tf_op jit(solution)/shard_map/reshape | solution.py:706
  6.1 0.0 copy-done
  6.1 1.3 copy.14
  7.5 282.3 %shard_map.122 = (bf16[256,1792]{1,0:T(8,128)(2,1)}, bf16[2,64,448]{2,1,0:T(8,128)(2,1)}) custom-call(bf16[256,1792]{1,0:T(8,128)(2,1)} %tokens_ref.1, f32[1792]{0:T(1024)} %norm_gain_ref.1, f32[1792]{0:T(1024)} %ffn_gain_ref.1, f32[3,448]{1,0:T(4,128)} %taps_ref.1, bf16[2,64,448]{2,1,0:T(8,128)(2,1)} %bitcast.10, s32[1]{0:T(128)S(6)} %copy.17.length_ref, ...), custom_call_target="tpu_custom_call" | custom-call | tf_op jit(solution)/shard_map/pallas_call | solution.py:655
  289.8 0.0 copy-start.1
  289.8 2.2 copy.18
  292.0 0.0 copy-done.1
  292.0 0.7 copy.19
Async XLA Ops:
  0.6 5.5 %copy-start = (bf16[224,2,1792]{2,1,0:T(2,128)(2,1)S(1)}, bf16[224,2,1792]{2,1,0:T(2,128)(2,1)}, u32[]{:S(2)}) copy-start(bf16[224,2,1792]{2,1,0:T(2,128)(2,1)} %param.16) | copy-start | bytes 4816900
  289.8 2.2 copy-start.1
